TPU v7x, 128 devices: a whole 4x4x4 slice. The times are simulated.
128 devices in a mesh: outer: 4 (over x_lo, core), inner: 32 (over y, x_hi, z).
Axes of the slice: x: 4 (x_hi: 2, x_lo: 2; x = x_hi * 2 + x_lo), y: 4, z: 4, core: 2. Of those that a mesh axis runs over, the one named last changes fastest.
Arguments:
- queries: bfloat16 [65536, 8, 128], P(('outer', 'inner')), may hold values from -162 to 162
- keys: bfloat16 [65536, 128], P(('outer', 'inner')), may hold values from -6 to 6
- values: bfloat16 [65536, 128], P(('outer', 'inner')), may hold values from -6 to 6
- grad_out: bfloat16 [65536, 8, 128], P(('outer', 'inner')), may hold values from -6 to 6
- doc_ids: int32 [65536], P(('outer', 'inner')), may hold values from 0 to 255, never falling along the last dimension, each value on 1 to 1536 neighbouring positions
Outputs:
- grad_queries: bfloat16 [65536, 8, 128], P(('outer', 'inner'))
- grad_keys: bfloat16 [65536, 128], P(('outer', 'inner'))
- grad_values: bfloat16 [65536, 128], P(('outer', 'inner'))
Inputs may be any that keep to these rules, and one draw needn't show every extreme that they name: `doc_ids`: documents are contiguous runs in the packed order, each of 1 to 1536 tokens, one of exactly 1536.
All inputs are finite; a program needn't handle non-finite values.
Results may differ from a plain program's by a relative error of at most 0.0054.
Values may be sent and summed in bfloat16 or wider, within the bound.
A program may use at most 256 MiB of HBM per device.

v0:
```python
import functools
import math

import jax
import jax.numpy as jnp
from jax import lax
from jax.experimental import pallas as pl
from jax.experimental.pallas import tpu as pltpu
from jax.sharding import PartitionSpec as P

REACH = 3
MESH = pl.DeviceIdType.MESH
BIG = 1.0e30
LANES = 128
TILE = 128
BF = jnp.bfloat16
F32 = jnp.float32


def nn(a, b):
    return lax.dot_general(a, b, (((1,), (0,)), ((), ())), preferred_element_type=F32)


def lane_groups(width):
    return [slice(j * LANES, (j + 1) * LANES) for j in range(width // LANES)]


def id_bits(ids, place):
    bit = lax.shift_right_logical(ids, place & 7) & 1
    return jnp.where(place < 8, bit, 1 - bit)


def three_pieces(x):
    first = x.astype(BF).astype(F32)
    second = (x - first).astype(BF).astype(F32)
    return first, second, x - first - second


def kernel(
    outer,
    inner,
    q_hbm,
    k_hbm,
    v_hbm,
    g_hbm,
    ids_ref,
    dq_hbm,
    dk_ref,
    dv_ref,
    kv,
    qa,
    ga,
    qt,
    gt,
    kat,
    vat,
    m_ref,
    l_ref,
    a_ref,
    dq_acc,
    dkt,
    dvt,
    part,
    got,
    dq_bf,
    load_sem,
    store_sem,
    send_sem,
    recv_sem,
    back_send_sem,
    back_recv_sem,
):
    tokens = k_hbm.shape[0]
    rows = q_hbm.shape[0]
    heads = rows // tokens
    tile_rows = TILE * heads
    tiles = tokens // TILE
    scale = LANES**-0.5
    to_log2 = scale * math.log2(math.e)
    count = outer * inner
    me = lax.axis_index("outer") * inner + lax.axis_index("inner")

    def device(delta):
        there = lax.rem(me + delta + count, count)
        return (there // inner, lax.rem(there, inner))

    barrier = pltpu.get_barrier_semaphore()
    for d in range(1, REACH + 1):
        for delta in (d, -d):
            pl.semaphore_signal(barrier, inc=1, device_id=device(delta), device_id_type=MESH)

    loads = [
        pltpu.make_async_copy(k_hbm, kv.at[0, pl.ds(0, tokens)], load_sem.at[0]),
        pltpu.make_async_copy(v_hbm, kv.at[0, pl.ds(tokens, tokens)], load_sem.at[1]),
        pltpu.make_async_copy(q_hbm, qa.at[:, pl.ds(0, LANES)], load_sem.at[2]),
        pltpu.make_async_copy(g_hbm, ga.at[:, pl.ds(0, LANES)], load_sem.at[3]),
    ]
    for copy in loads:
        copy.start()
    groups = tokens // LANES
    id_rows = jnp.concatenate(
        [ids_ref[...].astype(F32), jnp.zeros((16 - groups, LANES), F32)], axis=0
    )
    kv[0, pl.ds(2 * tokens, 16)] = id_rows.astype(BF)
    loads[0].wait()
    loads[1].wait()
    pl.semaphore_wait(barrier, 2 * REACH)

    def forward(d):
        return pltpu.make_async_remote_copy(
            src_ref=kv.at[0],
            dst_ref=kv.at[d],
            send_sem=send_sem.at[d],
            recv_sem=recv_sem.at[d],
            device_id=device(d),
            device_id_type=MESH,
        )

    def backward(d):
        return pltpu.make_async_remote_copy(
            src_ref=part.at[d],
            dst_ref=got.at[d],
            send_sem=back_send_sem.at[d],
            recv_sem=back_recv_sem.at[d],
            device_id=device(-d),
            device_id_type=MESH,
        )

    for d in range(1, REACH + 1):
        forward(d).start()

    lane = lax.broadcasted_iota(jnp.int32, (LANES, LANES), 1)
    sub = lax.broadcasted_iota(jnp.int32, (LANES, LANES), 0)
    own_ids = ids_ref[...].astype(F32)
    for t in range(tiles):
        ids_t = jnp.transpose(jnp.broadcast_to(own_ids[t : t + 1], (LANES, LANES)))
        feature = jnp.where(lane < 16, id_bits(ids_t.astype(jnp.int32), lane), 0).astype(F32)
        spread = jnp.broadcast_to(feature[:, None, :], (LANES, heads, LANES))
        qa[pl.ds(t * tile_rows, tile_rows), LANES:] = spread.reshape(tile_rows, LANES).astype(BF)

    def prepare_keys(d):
        kat[d, :LANES] = jnp.transpose(kv[d, pl.ds(0, tokens)])
        vat[d, :LANES] = jnp.transpose(kv[d, pl.ds(tokens, tokens)])
        ids = kv[d, pl.ds(2 * tokens, 16)].astype(F32)
        for j in range(groups):
            ids_j = jnp.broadcast_to(ids[j : j + 1], (LANES, LANES)).astype(jnp.int32)
            unequal = jnp.where(id_bits(ids_j, sub) == 1, 0.0, -BIG)
            ones = jnp.where(sub < 19, 1.0, 0.0)
            kat[d, LANES:, j * LANES : (j + 1) * LANES] = jnp.where(sub < 16, unequal, ones).astype(BF)
            vat[d, LANES:, j * LANES : (j + 1) * LANES] = jnp.where(sub < 3, 1.0, 0.0).astype(BF)

    tile_token = lax.broadcasted_iota(jnp.int32, (tile_rows, LANES), 0) // heads
    tile_key = lax.broadcasted_iota(jnp.int32, (tile_rows, LANES), 1)

    def pass_one(rows_at, d, keys_at, width, first, diagonal):
        scores = nn(qa[rows_at, :], kat[d, :, keys_at])
        dprob = nn(ga[rows_at, :LANES], vat[d, :LANES, keys_at])
        pieces = [scores[:, g] for g in lane_groups(width)]
        if diagonal:
            pieces[-1] = jnp.where(tile_key <= tile_token, pieces[-1], -BIG)
        top = functools.reduce(jnp.maximum, pieces)
        if not first:
            before = m_ref[rows_at, :]
            top = jnp.maximum(top, before)
            fade = jnp.exp2((before - top) * to_log2)
        m_ref[rows_at, :] = top
        norm = None if first else l_ref[rows_at, :] * fade
        total = None if first else a_ref[rows_at, :] * fade
        for piece, g in zip(pieces, lane_groups(width)):
            e = jnp.exp2((piece - top) * to_log2)
            ed = e * dprob[:, g]
            norm = e if norm is None else norm + e
            total = ed if total is None else total + ed
        l_ref[rows_at, :] = norm
        a_ref[rows_at, :] = total

    def pass_two(rows_at, d, keys_at, width, first, diagonal):
        shifted = nn(qa[rows_at, :], kat[d, :, keys_at])
        centred = nn(ga[rows_at, :], vat[d, :, keys_at])
        probs, dscores = [], []
        for j, g in enumerate(lane_groups(width)):
            x = shifted[:, g] * to_log2
            if diagonal and j == width // LANES - 1:
                x = jnp.where(tile_key <= tile_token, x, -BIG)
            p = jnp.exp2(x)
            probs.append(p.astype(BF))
            dscores.append((p * centred[:, g] * scale).astype(BF))
        probs = jnp.concatenate(probs, axis=1) if len(probs) > 1 else probs[0]
        dscores = jnp.concatenate(dscores, axis=1) if len(dscores) > 1 else dscores[0]
        dvt[:, keys_at] += nn(gt[:, rows_at], probs)
        dkt[:, keys_at] += nn(qt[:, rows_at], dscores)
        dq = nn(dscores, kv[d, keys_at, :])
        if first:
            dq_acc[rows_at, :] = dq
        else:
            dq_acc[rows_at, :] += dq

    def tile_at(t):
        return pl.ds(t * tile_rows, tile_rows)

    def whole_block(step, d):
        def one(t, carry):
            step(pl.ds(pl.multiple_of(t * tile_rows, tile_rows), tile_rows), d, pl.ds(0, tokens), tokens, False, False)
            return carry

        lax.fori_loop(0, tiles, one, 0)

    loads[2].wait()
    loads[3].wait()
    prepare_keys(0)
    for t in range(tiles):
        pass_one(tile_at(t), 0, pl.ds(0, (t + 1) * TILE), (t + 1) * TILE, True, True)
    for t in range(tiles):
        qt[:, tile_at(t)] = jnp.transpose(qa[tile_at(t), :LANES])
        gt[:, tile_at(t)] = jnp.transpose(ga[tile_at(t), :LANES])

    def near_one(step, carry):
        d = step + 1
        forward(d).wait_recv()
        prepare_keys(d)
        whole_block(pass_one, d)
        return carry

    lax.fori_loop(0, REACH - 1, near_one, 0)
    forward(REACH).wait_recv()
    prepare_keys(REACH)
    for t in range(tiles):
        pass_one(tile_at(t), REACH, pl.ds(t * TILE, tokens - t * TILE), tokens - t * TILE, False, False)

    wide_lane = lax.broadcasted_iota(jnp.int32, (tile_rows, LANES), 1)

    def normalise(t, carry):
        at = pl.ds(pl.multiple_of(t * tile_rows, tile_rows), tile_rows)
        m = m_ref[at, :]
        top = jnp.max(m, axis=1, keepdims=True)
        weight = jnp.exp2((m - top) * to_log2)
        norm = jnp.sum(l_ref[at, :] * weight, axis=1, keepdims=True)
        total = jnp.sum(a_ref[at, :] * weight, axis=1, keepdims=True)
        shift = -(top + jnp.log2(norm) * (1.0 / to_log2))
        delta = -total / norm
        s = three_pieces(shift)
        feature = qa[at, LANES:].astype(F32)
        for j in range(3):
            feature = jnp.where(wide_lane == 16 + j, s[j], feature)
        qa[at, LANES:] = feature.astype(BF)
        s = three_pieces(delta)
        feature = jnp.where(wide_lane == 0, s[0], jnp.where(wide_lane == 1, s[1], jnp.where(wide_lane == 2, s[2], 0.0)))
        ga[at, LANES:] = feature.astype(BF)
        return carry

    lax.fori_loop(0, tiles, normalise, 0)

    def clear():
        dkt[...] = jnp.zeros_like(dkt)
        dvt[...] = jnp.zeros_like(dvt)

    def send_parts(d):
        part[d, :LANES] = dkt[...].astype(BF)
        part[d, LANES:] = dvt[...].astype(BF)
        backward(d).start()

    clear()
    for t in range(tiles):
        pass_two(tile_at(t), REACH, pl.ds(t * TILE, tokens - t * TILE), tokens - t * TILE, True, False)
    send_parts(REACH)

    def near_two(step, carry):
        d = REACH - 1 - step
        clear()
        whole_block(pass_two, d)
        send_parts(d)
        return carry

    lax.fori_loop(0, REACH - 1, near_two, 0)
    clear()
    stores = []
    for t in range(tiles):
        pass_two(tile_at(t), 0, pl.ds(0, (t + 1) * TILE), (t + 1) * TILE, False, True)
        dq_bf[tile_at(t), :] = dq_acc[tile_at(t), :].astype(BF)
        stores.append(pltpu.make_async_copy(dq_bf.at[tile_at(t)], dq_hbm.at[tile_at(t)], store_sem.at[t]))
        stores[-1].start()

    key_total, val_total = dkt[...], dvt[...]
    for d in range(REACH, 0, -1):
        backward(d).wait_recv()
        key_total = key_total + got[d, :LANES].astype(F32)
        val_total = val_total + got[d, LANES:].astype(F32)
    dk_ref[...] = jnp.transpose(key_total).astype(BF)
    dv_ref[...] = jnp.transpose(val_total).astype(BF)
    for copy in stores:
        copy.wait()
    for d in range(1, REACH + 1):
        forward(d).wait_send()
        backward(d).wait_send()


def local(outer, inner, queries, keys, values, grad_out, doc_ids):
    tokens, heads, width = queries.shape
    rows = tokens * heads
    vmem = pltpu.VMEM
    slots = REACH + 1
    grad_queries, grad_keys, grad_values = pl.pallas_call(
        functools.partial(kernel, outer, inner),
        out_shape=(
            jax.ShapeDtypeStruct((rows, width), BF),
            jax.ShapeDtypeStruct((tokens, width), BF),
            jax.ShapeDtypeStruct((tokens, width), BF),
        ),
        in_specs=[pl.BlockSpec(memory_space=pl.ANY)] * 4 + [pl.BlockSpec(memory_space=vmem)],
        out_specs=(
            pl.BlockSpec(memory_space=pl.ANY),
            pl.BlockSpec(memory_space=vmem),
            pl.BlockSpec(memory_space=vmem),
        ),
        scratch_shapes=[
            vmem((slots, 2 * tokens + 16, width), BF),
            vmem((rows, 2 * width), BF),
            vmem((rows, 2 * width), BF),
            vmem((width, rows), BF),
            vmem((width, rows), BF),
            vmem((slots, 2 * width, tokens), BF),
            vmem((slots, 2 * width, tokens), BF),
            vmem((rows, width), F32),
            vmem((rows, width), F32),
            vmem((rows, width), F32),
            vmem((rows, width), F32),
            vmem((width, tokens), F32),
            vmem((width, tokens), F32),
            vmem((slots, 2 * width, tokens), BF),
            vmem((slots, 2 * width, tokens), BF),
            vmem((rows, width), BF),
            pltpu.SemaphoreType.DMA((4,)),
            pltpu.SemaphoreType.DMA((tokens // TILE,)),
            pltpu.SemaphoreType.DMA((slots,)),
            pltpu.SemaphoreType.DMA((slots,)),
            pltpu.SemaphoreType.DMA((slots,)),
            pltpu.SemaphoreType.DMA((slots,)),
        ],
        compiler_params=pltpu.CompilerParams(
            collective_id=0, has_side_effects=True, vmem_limit_bytes=56 * 2**20
        ),
        cost_estimate=pl.CostEstimate(
            flops=14 * rows * 1664 * width, bytes_accessed=8 * rows * width, transcendentals=2 * rows * 1664
        ),
    )(
        queries.reshape(rows, width),
        keys,
        values,
        grad_out.reshape(rows, width),
        doc_ids.reshape(tokens // LANES, LANES),
    )
    return grad_queries.reshape(queries.shape), grad_keys, grad_values


def solution(mesh):
    both = ("outer", "inner")
    return jax.shard_map(
        functools.partial(local, mesh.shape["outer"], mesh.shape["inner"]),
        mesh=mesh,
        in_specs=(P(both, None, None), P(both, None), P(both, None), P(both, None, None), P(both)),
        out_specs=(P(both, None, None), P(both, None), P(both, None)),
        check_vma=False,
    )
```

profile of v0, /device:TPU:110, one launch (start us, length us, event | category | flops | bytes accessed | tf_op | source)
XLA Modules:
  0.0 65.8 jit_solution(13580431233091429937)
XLA Ops:
  0.6 61.3 %shard_map.76 = (bf16[4096,128]{1,0:T(8,128)(2,1)}, bf16[512,128]{1,0:T(8,128)(2,1)}, bf16[512,128]{1,0:T(8,128)(2,1)}) custom-call(bf16[4096,128]{1,0:T(8,128)(2,1)} %bitcast.5, bf16[512,128]{1,0:T(8,128)(2,1)} %k_hbm.1, bf16[512,128]{1,0:T(8,128)(2,1)} %v_hbm.1, bf16[4096,128]{1,0:T(8,128)(2,1)} %bitcast.6, s32[4,128]{1,0:T(4,128)} %bitcast.7), custom_call_target="tpu_custom_call" | custom-call | flops 12213813248 | bytes 4194304 | tf_op jit(solution)/shard_map/pallas_call | solution.py:302
  61.9 0.0 copy-start.1
  61.9 2.3 %copy.11 = bf16[512,8,128]{2,1,0:T(8,128)(2,1)} copy(bf16[512,8,128]{2,1,0:T(8,128)(2,1)} %bitcast.4) | data formatting | bytes 2097152
  64.2 0.0 copy-done.1
  64.2 0.0 copy-start
  64.2 0.7 copy.12
  64.9 0.3 copy-done
  65.2 0.7 copy.13
Async XLA Ops:
  61.9 2.3 %copy-start.1 = (bf16[512,128]{1,0:T(8,128)(2,1)S(1)}, bf16[512,128]{1,0:T(8,128)(2,1)}, u32[]{:S(2)}) copy-start(bf16[512,128]{1,0:T(8,128)(2,1)} %get-tuple-element.13) | copy-start | bytes 393220
  64.2 1.0 %copy-start = (bf16[512,128]{1,0:T(8,128)(2,1)S(1)}, bf16[512,128]{1,0:T(8,128)(2,1)}, u32[]{:S(2)}) copy-start(bf16[512,128]{1,0:T(8,128)(2,1)} %get-tuple-element.14) | copy-start | bytes 393220
where the time goes:
time: 66 us; the launch traced here: 65.8 us
  Pallas kernels  61.3 us (93%)
  local copies, waits for them, and re-layouts  3.91 us (6%)
    pallas_call x1, Pallas kernels, local(): pl.pallas_call(functools.partial(kernel, outer, inner), out_shape=(jax.Sh...  61.3 us
    unnamed x7, local copies, waits for them, and re-layouts  3.91 us

commit v1 on v0

v1 whole, which is shorter than its diff:
```python
import functools
import math

import jax
import jax.numpy as jnp
from jax import lax
from jax.experimental import pallas as pl
from jax.experimental.pallas import tpu as pltpu
from jax.sharding import PartitionSpec as P

REACH = 3
MESH = pl.DeviceIdType.MESH
BIG = 1.0e30
LANES = 128
TILE = 128
SEND_ORDER = ((0, 1), (0, 2), (0, 3), (1, 1), (1, 2), (1, 3))
BF = jnp.bfloat16
F32 = jnp.float32


def nn(a, b):
    return lax.dot_general(a, b, (((1,), (0,)), ((), ())), preferred_element_type=F32)


def lane_groups(width):
    return [slice(j * LANES, (j + 1) * LANES) for j in range(width // LANES)]


def id_bits(ids, place):
    bit = lax.shift_right_logical(ids, place & 7) & 1
    return jnp.where(place < 8, bit, 1 - bit)


def three_pieces(x):
    first = x.astype(BF).astype(F32)
    second = (x - first).astype(BF).astype(F32)
    return first, second, x - first - second


def kernel(
    outer,
    inner,
    q_hbm,
    k_hbm,
    v_hbm,
    g_hbm,
    ids_ref,
    dq_hbm,
    dk_ref,
    dv_ref,
    kv,
    qa,
    ga,
    qt,
    gt,
    kat,
    vat,
    s_mid,
    s_edge,
    m_ref,
    l_ref,
    dq_acc,
    dkt,
    dvt,
    part,
    got,
    dq_bf,
    load_sem,
    store_sem,
    send_sem,
    recv_sem,
    back_send_sem,
    back_recv_sem,
):
    tokens = k_hbm.shape[0]
    rows = q_hbm.shape[0]
    heads = rows // tokens
    tile_rows = TILE * heads
    tiles = tokens // TILE
    scale = LANES**-0.5
    to_log2 = scale * math.log2(math.e)
    count = outer * inner
    me = lax.axis_index("outer") * inner + lax.axis_index("inner")

    def device(delta):
        there = lax.rem(me + delta + count, count)
        return (there // inner, lax.rem(there, inner))

    barrier = pltpu.get_barrier_semaphore()
    for d in range(1, REACH + 1):
        for delta in (d, -d):
            pl.semaphore_signal(barrier, inc=1, device_id=device(delta), device_id_type=MESH)

    loads = [
        pltpu.make_async_copy(k_hbm, kv.at[0, pl.ds(tokens, tokens)], load_sem.at[0]),
        pltpu.make_async_copy(v_hbm, kv.at[0, pl.ds(0, tokens)], load_sem.at[1]),
        pltpu.make_async_copy(q_hbm, qa.at[:, pl.ds(0, LANES)], load_sem.at[2]),
        pltpu.make_async_copy(g_hbm, ga.at[:, pl.ds(0, LANES)], load_sem.at[3]),
    ]
    for copy in loads:
        copy.start()
    groups = tokens // LANES
    id_rows = jnp.concatenate(
        [ids_ref[...].astype(F32), jnp.zeros((16 - groups, LANES), F32)], axis=0
    )
    kv[0, pl.ds(2 * tokens, 16)] = id_rows.astype(BF)
    loads[0].wait()
    loads[1].wait()
    pl.semaphore_wait(barrier, 2 * REACH)

    def forward(half, d):
        at = pl.ds(tokens, tokens + 16) if half == 0 else pl.ds(0, tokens)
        return pltpu.make_async_remote_copy(
            src_ref=kv.at[0, at],
            dst_ref=kv.at[d, at],
            send_sem=send_sem.at[half, d],
            recv_sem=recv_sem.at[half, d],
            device_id=device(d),
            device_id_type=MESH,
        )

    def backward(half, d):
        return pltpu.make_async_remote_copy(
            src_ref=part.at[half, d],
            dst_ref=got.at[half, d],
            send_sem=back_send_sem.at[half, d],
            recv_sem=back_recv_sem.at[half, d],
            device_id=device(-d),
            device_id_type=MESH,
        )

    for half, d in SEND_ORDER:
        forward(half, d).start()

    lane = lax.broadcasted_iota(jnp.int32, (LANES, LANES), 1)
    sub = lax.broadcasted_iota(jnp.int32, (LANES, LANES), 0)
    own_ids = ids_ref[...].astype(F32)
    for t in range(tiles):
        ids_t = jnp.transpose(jnp.broadcast_to(own_ids[t : t + 1], (LANES, LANES)))
        feature = jnp.where(lane < 16, id_bits(ids_t.astype(jnp.int32), lane), 0).astype(F32)
        spread = jnp.broadcast_to(feature[:, None, :], (LANES, heads, LANES))
        qa[pl.ds(t * tile_rows, tile_rows), LANES:] = spread.reshape(tile_rows, LANES).astype(BF)

    def prepare_keys(d):
        kat[d, :LANES] = jnp.transpose(kv[d, pl.ds(tokens, tokens)])
        ids = kv[d, pl.ds(2 * tokens, 16)].astype(F32)
        for j in range(groups):
            ids_j = jnp.broadcast_to(ids[j : j + 1], (LANES, LANES)).astype(jnp.int32)
            unequal = jnp.where((id_bits(ids_j, sub) == 0) & (sub < 16), -BIG, 0.0)
            kat[d, LANES:, j * LANES : (j + 1) * LANES] = unequal.astype(BF)

    def prepare_values(d):
        vat[d, :LANES] = jnp.transpose(kv[d, pl.ds(0, tokens)])
        ones = jnp.where(lax.broadcasted_iota(jnp.int32, (LANES, tokens), 0) < 3, 1.0, 0.0)
        vat[d, LANES:] = ones.astype(BF)

    tile_token = lax.broadcasted_iota(jnp.int32, (tile_rows, LANES), 0) // heads
    tile_key = lax.broadcasted_iota(jnp.int32, (tile_rows, LANES), 1)

    def tile_at(t):
        return pl.ds(t * tile_rows, tile_rows)

    def keys_of(d, t):
        if d == 0:
            return 0, (t + 1) * TILE
        if d == REACH:
            return t * TILE, tokens - t * TILE
        return 0, tokens

    def stored(d, t):
        if d == 0:
            return s_edge.at[tile_at(t), pl.ds(0, (t + 1) * TILE)]
        if d == REACH:
            return s_edge.at[tile_at(t), pl.ds((t + 1) * TILE, tokens - t * TILE)]
        return s_mid.at[d - 1, tile_at(t)]

    def score_tile(d, t):
        rows_at = tile_at(t)
        start, width = keys_of(d, t)
        scores = nn(qa[rows_at, :], kat[d, :, pl.ds(start, width)])
        pieces = [scores[:, g] for g in lane_groups(width)]
        if d == 0:
            pieces[-1] = jnp.where(tile_key <= tile_token, pieces[-1], -BIG)
        top = functools.reduce(jnp.maximum, pieces)
        norm = None
        if d > 0:
            before = m_ref[rows_at, :]
            top = jnp.maximum(top, before)
            norm = l_ref[rows_at, :] * jnp.exp2((before - top) * to_log2)
        m_ref[rows_at, :] = top
        place = stored(d, t)
        for piece, g in zip(pieces, lane_groups(width)):
            place[:, g] = piece
            e = jnp.exp2((piece - top) * to_log2)
            norm = e if norm is None else norm + e
        l_ref[rows_at, :] = norm

    def log_norm_tile(t):
        rows_at = tile_at(t)
        m = m_ref[rows_at, :]
        top = jnp.max(m, axis=1, keepdims=True)
        norm = jnp.sum(l_ref[rows_at, :] * jnp.exp2((m - top) * to_log2), axis=1, keepdims=True)
        m_ref[rows_at, :] = jnp.broadcast_to(top * to_log2 + jnp.log2(norm), (tile_rows, LANES))

    def value_tile(d, t):
        rows_at = tile_at(t)
        start, width = keys_of(d, t)
        log_norm = m_ref[rows_at, :]
        place = stored(d, t)
        probs = []
        for g in lane_groups(width):
            p = jnp.exp2(place[:, g] * to_log2 - log_norm)
            place[:, g] = p
            probs.append(p.astype(BF))
        probs = jnp.concatenate(probs, axis=1) if len(probs) > 1 else probs[0]
        dvt[:, pl.ds(start, width)] += nn(gt[:, rows_at], probs)

    def delta_tile(d, t):
        rows_at = tile_at(t)
        start, width = keys_of(d, t)
        dprob = nn(ga[rows_at, :LANES], vat[d, :LANES, pl.ds(start, width)])
        place = stored(d, t)
        total = None if d == 0 else l_ref[rows_at, :]
        for g in lane_groups(width):
            pd = place[:, g] * dprob[:, g]
            total = pd if total is None else total + pd
        l_ref[rows_at, :] = total

    def delta_feature_tile(t):
        rows_at = tile_at(t)
        pieces = three_pieces(-jnp.sum(l_ref[rows_at, :], axis=1, keepdims=True))
        feature = jnp.zeros((tile_rows, LANES), F32)
        for j, piece in enumerate(pieces):
            feature = jnp.where(tile_key == j, piece, feature)
        ga[rows_at, LANES:] = feature.astype(BF)

    def key_tile(d, t):
        rows_at = tile_at(t)
        start, width = keys_of(d, t)
        centred = nn(ga[rows_at, :], vat[d, :, pl.ds(start, width)])
        place = stored(d, t)
        dscores = [(place[:, g] * centred[:, g] * scale).astype(BF) for g in lane_groups(width)]
        dscores = jnp.concatenate(dscores, axis=1) if len(dscores) > 1 else dscores[0]
        dkt[:, pl.ds(start, width)] += nn(qt[:, rows_at], dscores)
        dq = nn(dscores, kv[d, pl.ds(tokens + start, width), :])
        if d == REACH:
            dq_acc[rows_at, :] = dq
        elif d > 0:
            dq_acc[rows_at, :] += dq
        else:
            dq_bf[rows_at, :] = (dq_acc[rows_at, :] + dq).astype(BF)

    loads[2].wait()
    loads[3].wait()
    prepare_keys(0)
    prepare_values(0)
    for t in range(tiles):
        score_tile(0, t)
    for t in range(tiles):
        qt[:, tile_at(t)] = jnp.transpose(qa[tile_at(t), :LANES])
        gt[:, tile_at(t)] = jnp.transpose(ga[tile_at(t), :LANES])
    for d in range(1, REACH + 1):
        forward(0, d).wait_recv()
        prepare_keys(d)
        for t in range(tiles):
            score_tile(d, t)
    for t in range(tiles):
        log_norm_tile(t)

    for d in range(REACH, -1, -1):
        dvt[...] = jnp.zeros_like(dvt)
        for t in range(tiles):
            value_tile(d, t)
        if d > 0:
            part[1, d] = dvt[...].astype(BF)
            backward(1, d).start()

    for d in range(REACH + 1):
        if d > 0:
            forward(1, d).wait_recv()
            prepare_values(d)
        for t in range(tiles):
            delta_tile(d, t)
    for t in range(tiles):
        delta_feature_tile(t)

    stores = []
    for d in range(REACH, -1, -1):
        dkt[...] = jnp.zeros_like(dkt)
        if d == 0:
            val_total = dvt[...]
            for b in range(REACH, 0, -1):
                backward(1, b).wait_recv()
                val_total = val_total + got[1, b].astype(F32)
            dv_ref[...] = jnp.transpose(val_total).astype(BF)
        for t in range(tiles):
            key_tile(d, t)
            if d == 0:
                stores.append(pltpu.make_async_copy(dq_bf.at[tile_at(t)], dq_hbm.at[tile_at(t)], store_sem.at[t]))
                stores[-1].start()
        if d > 0:
            part[0, d] = dkt[...].astype(BF)
            backward(0, d).start()

    key_total = dkt[...]
    for d in range(REACH, 0, -1):
        backward(0, d).wait_recv()
        key_total = key_total + got[0, d].astype(F32)
    dk_ref[...] = jnp.transpose(key_total).astype(BF)
    for copy in stores:
        copy.wait()
    for d in range(1, REACH + 1):
        for half in range(2):
            forward(half, d).wait_send()
            backward(half, d).wait_send()


def local(outer, inner, queries, keys, values, grad_out, doc_ids):
    tokens, heads, width = queries.shape
    rows = tokens * heads
    vmem = pltpu.VMEM
    slots = REACH + 1
    grad_queries, grad_keys, grad_values = pl.pallas_call(
        functools.partial(kernel, outer, inner),
        out_shape=(
            jax.ShapeDtypeStruct((rows, width), BF),
            jax.ShapeDtypeStruct((tokens, width), BF),
            jax.ShapeDtypeStruct((tokens, width), BF),
        ),
        in_specs=[pl.BlockSpec(memory_space=pl.ANY)] * 4 + [pl.BlockSpec(memory_space=vmem)],
        out_specs=(
            pl.BlockSpec(memory_space=pl.ANY),
            pl.BlockSpec(memory_space=vmem),
            pl.BlockSpec(memory_space=vmem),
        ),
        scratch_shapes=[
            vmem((slots, 2 * tokens + 16, width), BF),
            vmem((rows, 2 * width), BF),
            vmem((rows, 2 * width), BF),
            vmem((width, rows), BF),
            vmem((width, rows), BF),
            vmem((slots, 2 * width, tokens), BF),
            vmem((slots, 2 * width, tokens), BF),
            vmem((REACH - 1, rows, tokens), F32),
            vmem((rows, tokens + TILE), F32),
            vmem((rows, width), F32),
            vmem((rows, width), F32),
            vmem((rows, width), F32),
            vmem((width, tokens), F32),
            vmem((width, tokens), F32),
            vmem((2, slots, width, tokens), BF),
            vmem((2, slots, width, tokens), BF),
            vmem((rows, width), BF),
            pltpu.SemaphoreType.DMA((4,)),
            pltpu.SemaphoreType.DMA((tokens // TILE,)),
            pltpu.SemaphoreType.DMA((2, slots)),
            pltpu.SemaphoreType.DMA((2, slots)),
            pltpu.SemaphoreType.DMA((2, slots)),
            pltpu.SemaphoreType.DMA((2, slots)),
        ],
        compiler_params=pltpu.CompilerParams(
            collective_id=0, has_side_effects=True, vmem_limit_bytes=60 * 2**20
        ),
        cost_estimate=pl.CostEstimate(
            flops=12 * rows * 1664 * width, bytes_accessed=8 * rows * width, transcendentals=2 * rows * 1664
        ),
    )(
        queries.reshape(rows, width),
        keys,
        values,
        grad_out.reshape(rows, width),
        doc_ids.reshape(tokens // LANES, LANES),
    )
    return grad_queries.reshape(queries.shape), grad_keys, grad_values


def solution(mesh):
    both = ("outer", "inner")
    return jax.shard_map(
        functools.partial(local, mesh.shape["outer"], mesh.shape["inner"]),
        mesh=mesh,
        in_specs=(P(both, None, None), P(both, None), P(both, None), P(both, None, None), P(both)),
        out_specs=(P(both, None, None), P(both, None), P(both, None)),
        check_vma=False,
    )
```

time: 66 us -> 54.8 us (0.83)
  the two profiles are of different devices: /device:TPU:110 before, /device:TPU:0 now
where the time goes in v1:
time: 54.8 us; the launch traced here: 54.6 us
  Pallas kernels  50 us (91%)
  local copies, waits for them, and re-layouts  3.91 us (7%)
  between operations  0.65 us (1%)
    pallas_call x1, Pallas kernels, local(): pl.pallas_call(functools.partial(kernel, outer, inner), out_shape=(jax.Sh...  50 us
    unnamed x7, local copies, waits for them, and re-layouts  3.91 us

profile of v1, /device:TPU:0, one launch (start us, length us, event | category | flops | bytes accessed | tf_op | source)
XLA Modules:
  0.0 54.6 jit_solution(14660985666819510577)
XLA Ops:
  0.6 50.0 %shard_map.76 = (bf16[4096,128]{1,0:T(8,128)(2,1)}, bf16[512,128]{1,0:T(8,128)(2,1)}, bf16[512,128]{1,0:T(8,128)(2,1)}) custom-call(bf16[4096,128]{1,0:T(8,128)(2,1)} %bitcast.5, bf16[512,128]{1,0:T(8,128)(2,1)} %k_hbm.1, bf16[512,128]{1,0:T(8,128)(2,1)} %v_hbm.1, bf16[4096,128]{1,0:T(8,128)(2,1)} %bitcast.6, s32[4,128]{1,0:T(4,128)} %bitcast.7), custom_call_target="tpu_custom_call" | custom-call | flops 10468982784 | bytes 4194304 | tf_op jit(solution)/shard_map/pallas_call | solution.py:323
  50.7 0.0 copy-start.1
  50.7 2.3 %copy.11 = bf16[512,8,128]{2,1,0:T(8,128)(2,1)} copy(bf16[512,8,128]{2,1,0:T(8,128)(2,1)} %bitcast.4) | data formatting | bytes 2097152
  53.0 0.0 copy-done.1
  53.0 0.0 copy-start
  53.0 0.7 %copy.12 = bf16[512,128]{1,0:T(8,128)(2,1)} copy(bf16[512,128]{1,0:T(8,128)(2,1)S(1)} %copy-done.1) | data formatting | bytes 262144
  53.6 0.3 copy-done
  53.9 0.7 %copy.13 = bf16[512,128]{1,0:T(8,128)(2,1)} copy(bf16[512,128]{1,0:T(8,128)(2,1)S(1)} %copy-done) | data formatting | bytes 262144
Async XLA Ops:
  50.7 2.3 %copy-start.1 = (bf16[512,128]{1,0:T(8,128)(2,1)S(1)}, bf16[512,128]{1,0:T(8,128)(2,1)}, u32[]{:S(2)}) copy-start(bf16[512,128]{1,0:T(8,128)(2,1)} %get-tuple-element.13) | copy-start | bytes 393220
  53.0 1.0 %copy-start = (bf16[512,128]{1,0:T(8,128)(2,1)S(1)}, bf16[512,128]{1,0:T(8,128)(2,1)}, u32[]{:S(2)}) copy-start(bf16[512,128]{1,0:T(8,128)(2,1)} %get-tuple-element.14) | copy-start | bytes 393220

commit v2 on v1

--- a/solution.py
+++ b/solution.py
@@ -60,7 +60,6 @@
     m_ref,
     l_ref,
     dq_acc,
-    dkt,
     dvt,
     part,
     got,
@@ -135,11 +134,12 @@
     lane = lax.broadcasted_iota(jnp.int32, (LANES, LANES), 1)
     sub = lax.broadcasted_iota(jnp.int32, (LANES, LANES), 0)
     own_ids = ids_ref[...].astype(F32)
-    for t in range(tiles):
+    for t in range(groups):
         ids_t = jnp.transpose(jnp.broadcast_to(own_ids[t : t + 1], (LANES, LANES)))
         feature = jnp.where(lane < 16, id_bits(ids_t.astype(jnp.int32), lane), 0).astype(F32)
         spread = jnp.broadcast_to(feature[:, None, :], (LANES, heads, LANES))
-        qa[pl.ds(t * tile_rows, tile_rows), LANES:] = spread.reshape(tile_rows, LANES).astype(BF)
+        at = pl.ds(t * LANES * heads, LANES * heads)
+        qa[at, LANES:] = spread.reshape(LANES * heads, LANES).astype(BF)
 
     def prepare_keys(d):
         kat[d, :LANES] = jnp.transpose(kv[d, pl.ds(tokens, tokens)])
@@ -180,7 +180,9 @@
         scores = nn(qa[rows_at, :], kat[d, :, pl.ds(start, width)])
         pieces = [scores[:, g] for g in lane_groups(width)]
         if d == 0:
-            pieces[-1] = jnp.where(tile_key <= tile_token, pieces[-1], -BIG)
+            for j in range(TILE // LANES):
+                k = j - TILE // LANES
+                pieces[k] = jnp.where(tile_key + j * LANES <= tile_token, pieces[k], -BIG)
         top = functools.reduce(jnp.maximum, pieces)
         norm = None
         if d > 0:
@@ -205,26 +207,20 @@
     def value_tile(d, t):
         rows_at = tile_at(t)
         start, width = keys_of(d, t)
+        dprob = nn(ga[rows_at, :LANES], vat[d, :LANES, pl.ds(start, width)])
         log_norm = m_ref[rows_at, :]
         place = stored(d, t)
+        total = None if d == 0 else l_ref[rows_at, :]
         probs = []
         for g in lane_groups(width):
             p = jnp.exp2(place[:, g] * to_log2 - log_norm)
             place[:, g] = p
             probs.append(p.astype(BF))
-        probs = jnp.concatenate(probs, axis=1) if len(probs) > 1 else probs[0]
-        dvt[:, pl.ds(start, width)] += nn(gt[:, rows_at], probs)
-
-    def delta_tile(d, t):
-        rows_at = tile_at(t)
-        start, width = keys_of(d, t)
-        dprob = nn(ga[rows_at, :LANES], vat[d, :LANES, pl.ds(start, width)])
-        place = stored(d, t)
-        total = None if d == 0 else l_ref[rows_at, :]
-        for g in lane_groups(width):
-            pd = place[:, g] * dprob[:, g]
+            pd = p * dprob[:, g]
             total = pd if total is None else total + pd
         l_ref[rows_at, :] = total
+        probs = jnp.concatenate(probs, axis=1) if len(probs) > 1 else probs[0]
+        return nn(gt[:, rows_at], probs)
 
     def delta_feature_tile(t):
         rows_at = tile_at(t)
@@ -241,7 +237,7 @@
         place = stored(d, t)
         dscores = [(place[:, g] * centred[:, g] * scale).astype(BF) for g in lane_groups(width)]
         dscores = jnp.concatenate(dscores, axis=1) if len(dscores) > 1 else dscores[0]
-        dkt[:, pl.ds(start, width)] += nn(qt[:, rows_at], dscores)
+        key_sum = nn(qt[:, rows_at], dscores)
         dq = nn(dscores, kv[d, pl.ds(tokens + start, width), :])
         if d == REACH:
             dq_acc[rows_at, :] = dq
@@ -249,6 +245,13 @@
             dq_acc[rows_at, :] += dq
         else:
             dq_bf[rows_at, :] = (dq_acc[rows_at, :] + dq).astype(BF)
+        return key_sum
+
+    def add_up(sums, d, t, term):
+        start, width = keys_of(d, t)
+        for j, g in enumerate(lane_groups(width)):
+            at = start // LANES + j
+            sums[at] = term[:, g] if sums[at] is None else sums[at] + term[:, g]
 
     loads[2].wait()
     loads[3].wait()
@@ -267,26 +270,27 @@
     for t in range(tiles):
         log_norm_tile(t)
 
-    for d in range(REACH, -1, -1):
-        dvt[...] = jnp.zeros_like(dvt)
-        for t in range(tiles):
-            value_tile(d, t)
-        if d > 0:
-            part[1, d] = dvt[...].astype(BF)
-            backward(1, d).start()
-
     for d in range(REACH + 1):
         if d > 0:
             forward(1, d).wait_recv()
             prepare_values(d)
+        sums = [None] * groups
         for t in range(tiles):
-            delta_tile(d, t)
+            add_up(sums, d, t, value_tile(d, t))
+        for j, g in enumerate(lane_groups(tokens)):
+            if d > 0:
+                part[1, d, :, g] = sums[j].astype(BF)
+            else:
+                dvt[:, g] = sums[j]
+        if d > 0:
+            backward(1, d).start()
+
     for t in range(tiles):
         delta_feature_tile(t)
 
     stores = []
     for d in range(REACH, -1, -1):
-        dkt[...] = jnp.zeros_like(dkt)
+        sums = [None] * groups
         if d == 0:
             val_total = dvt[...]
             for b in range(REACH, 0, -1):
@@ -294,15 +298,16 @@
                 val_total = val_total + got[1, b].astype(F32)
             dv_ref[...] = jnp.transpose(val_total).astype(BF)
         for t in range(tiles):
-            key_tile(d, t)
+            add_up(sums, d, t, key_tile(d, t))
             if d == 0:
                 stores.append(pltpu.make_async_copy(dq_bf.at[tile_at(t)], dq_hbm.at[tile_at(t)], store_sem.at[t]))
                 stores[-1].start()
         if d > 0:
-            part[0, d] = dkt[...].astype(BF)
+            for j, g in enumerate(lane_groups(tokens)):
+                part[0, d, :, g] = sums[j].astype(BF)
             backward(0, d).start()
 
-    key_total = dkt[...]
+    key_total = jnp.concatenate(sums, axis=1)
     for d in range(REACH, 0, -1):
         backward(0, d).wait_recv()
         key_total = key_total + got[0, d].astype(F32)
@@ -313,6 +318,11 @@
         for half in range(2):
             forward(half, d).wait_send()
             backward(half, d).wait_send()
+
+
+def finish(dq_in, dk_in, dv_in, dq_out, dk_out, dv_out):
+    for taken, given in ((dq_in, dq_out), (dk_in, dk_out), (dv_in, dv_out)):
+        given[...] = taken[...]
 
 
 def local(outer, inner, queries, keys, values, grad_out, doc_ids):
@@ -347,7 +357,6 @@
             vmem((rows, width), F32),
             vmem((rows, width), F32),
             vmem((width, tokens), F32),
-            vmem((width, tokens), F32),
             vmem((2, slots, width, tokens), BF),
             vmem((2, slots, width, tokens), BF),
             vmem((rows, width), BF),
@@ -371,6 +380,16 @@
         grad_out.reshape(rows, width),
         doc_ids.reshape(tokens // LANES, LANES),
     )
+    grad_queries, grad_keys, grad_values = pl.pallas_call(
+        finish,
+        out_shape=(
+            jax.ShapeDtypeStruct((rows, width), BF),
+            jax.ShapeDtypeStruct((tokens, width), BF),
+            jax.ShapeDtypeStruct((tokens, width), BF),
+        ),
+        in_specs=[pl.BlockSpec(memory_space=vmem)] * 3,
+        out_specs=[pl.BlockSpec(memory_space=vmem)] * 3,
+    )(grad_queries, grad_keys, grad_values)
     return grad_queries.reshape(queries.shape), grad_keys, grad_values
 
 

time: 54.8 us -> 52.2 us (0.953)
  local copies, waits for them, and re-layouts: 3.91 us -> 0 us
  Pallas kernels: 50 us -> 51.4 us
    unnamed x7 -> x0, local copies, waits for them, and re-layouts: 3.91 us -> none
    pallas_call x0 -> x1, Pallas kernels: none -> 2.38 us  [local(): pl.pallas_call(finish, out_shape=(jax.ShapeDtypeStruct((rows, width), BF)...]
    pallas_call x1, Pallas kernels: 50 us -> 49 us  [local(): pl.pallas_call(functools.partial(kernel, outer, inner), out_shape=(jax.Sh...]
where the time goes in v2:
time: 52.2 us; the launch traced here: 52 us
  Pallas kernels  51.4 us (98%)
  between operations  0.64 us (1%)
    pallas_call x1, Pallas kernels, local(): pl.pallas_call(functools.partial(kernel, outer, inner), out_shape=(jax.Sh...  49 us
    pallas_call x1, Pallas kernels, local(): pl.pallas_call(finish, out_shape=(jax.ShapeDtypeStruct((rows, width), BF)...  2.38 us

profile of v2, /device:TPU:0, one launch (start us, length us, event | category | flops | bytes accessed | tf_op | source)
XLA Modules:
  0.0 52.0 jit_solution(11786568902476897238)
XLA Ops:
  0.6 49.0 %shard_map.76 = (bf16[4096,128]{1,0:T(8,128)(2,1)}, bf16[512,128]{1,0:T(8,128)(2,1)}, bf16[512,128]{1,0:T(8,128)(2,1)}) custom-call(bf16[4096,128]{1,0:T(8,128)(2,1)} %bitcast.4, bf16[512,128]{1,0:T(8,128)(2,1)} %k_hbm.1, bf16[512,128]{1,0:T(8,128)(2,1)} %v_hbm.1, bf16[4096,128]{1,0:T(8,128)(2,1)} %bitcast.5, s32[4,128]{1,0:T(4,128)} %bitcast.7), custom_call_target="tpu_custom_call" | custom-call | flops 10468982784 | bytes 4194304 | tf_op jit(solution)/shard_map/pallas_call | solution.py:333
  49.6 2.4 %shard_map.77 = (bf16[4096,128]{1,0:T(8,128)(2,1)}, bf16[512,128]{1,0:T(8,128)(2,1)}, bf16[512,128]{1,0:T(8,128)(2,1)}) custom-call(bf16[4096,128]{1,0:T(8,128)(2,1)} %get-tuple-element.9.dq_in, bf16[512,128]{1,0:T(8,128)(2,1)} %get-tuple-element.10.dk_in, bf16[512,128]{1,0:T(8,128)(2,1)} %get-tuple-element.11.dv_in), custom_call_target="tpu_custom_call" | custom-call | tf_op jit(solution)/shard_map/pallas_call | solution.py:383

commit v3 on v2

--- a/solution.py
+++ b/solution.py
@@ -13,7 +13,7 @@
 BIG = 1.0e30
 LANES = 128
 TILE = 128
-SEND_ORDER = ((0, 1), (0, 2), (0, 3), (1, 1), (1, 2), (1, 3))
+SEND_ORDER = ((2, 1), (2, 2), (2, 3), (0, 1), (0, 2), (0, 3), (1, 1), (1, 2), (1, 3))
 BF = jnp.bfloat16
 F32 = jnp.float32
 
@@ -103,14 +103,12 @@
         [ids_ref[...].astype(F32), jnp.zeros((16 - groups, LANES), F32)], axis=0
     )
     kv[0, pl.ds(2 * tokens, 16)] = id_rows.astype(BF)
-    loads[0].wait()
-    loads[1].wait()
     pl.semaphore_wait(barrier, 2 * REACH)
 
     def forward(half, d):
-        at = pl.ds(tokens, tokens + 16) if half == 0 else pl.ds(0, tokens)
+        at = (pl.ds(tokens, tokens), pl.ds(0, tokens), pl.ds(2 * tokens, 16))[half]
         return pltpu.make_async_remote_copy(
-            src_ref=kv.at[0, at],
+            src_ref=k_hbm if half == 0 else kv.at[0, at],
             dst_ref=kv.at[d, at],
             send_sem=send_sem.at[half, d],
             recv_sem=recv_sem.at[half, d],
@@ -129,6 +127,8 @@
         )
 
     for half, d in SEND_ORDER:
+        if (half, d) == (1, 1):
+            loads[1].wait()
         forward(half, d).start()
 
     lane = lax.broadcasted_iota(jnp.int32, (LANES, LANES), 1)
@@ -253,8 +253,8 @@
             at = start // LANES + j
             sums[at] = term[:, g] if sums[at] is None else sums[at] + term[:, g]
 
-    loads[2].wait()
-    loads[3].wait()
+    for copy in (loads[0], loads[2], loads[3]):
+        copy.wait()
     prepare_keys(0)
     prepare_values(0)
     for t in range(tiles):
@@ -263,6 +263,7 @@
         qt[:, tile_at(t)] = jnp.transpose(qa[tile_at(t), :LANES])
         gt[:, tile_at(t)] = jnp.transpose(ga[tile_at(t), :LANES])
     for d in range(1, REACH + 1):
+        forward(2, d).wait_recv()
         forward(0, d).wait_recv()
         prepare_keys(d)
         for t in range(tiles):
@@ -318,6 +319,7 @@
         for half in range(2):
             forward(half, d).wait_send()
             backward(half, d).wait_send()
+        forward(2, d).wait_send()
 
 
 def finish(dq_in, dk_in, dv_in, dq_out, dk_out, dv_out):
@@ -362,8 +364,8 @@
             vmem((rows, width), BF),
             pltpu.SemaphoreType.DMA((4,)),
             pltpu.SemaphoreType.DMA((tokens // TILE,)),
-            pltpu.SemaphoreType.DMA((2, slots)),
-            pltpu.SemaphoreType.DMA((2, slots)),
+            pltpu.SemaphoreType.DMA((3, slots)),
+            pltpu.SemaphoreType.DMA((3, slots)),
             pltpu.SemaphoreType.DMA((2, slots)),
             pltpu.SemaphoreType.DMA((2, slots)),
         ],

time: 52.2 us -> 51.1 us (0.979)
  Pallas kernels: 51.4 us -> 50.3 us
    pallas_call x1, Pallas kernels: 49 us -> 47.9 us  [local(): pl.pallas_call(functools.partial(kernel, outer, inner), out_shape=(jax.Sh...]
where the time goes in v3:
time: 51.1 us; the launch traced here: 50.9 us
  Pallas kernels  50.3 us (98%)
  between operations  0.64 us (1%)
    pallas_call x1, Pallas kernels, local(): pl.pallas_call(functools.partial(kernel, outer, inner), out_shape=(jax.Sh...  47.9 us
    pallas_call x1, Pallas kernels, local(): pl.pallas_call(finish, out_shape=(jax.ShapeDtypeStruct((rows, width), BF)...  2.38 us

profile of v3, /device:TPU:0, one launch (start us, length us, event | category | flops | bytes accessed | tf_op | source)
XLA Modules:
  0.0 50.9 jit_solution(7662132384534456644)
XLA Ops:
  0.6 47.9 %shard_map.76 = (bf16[4096,128]{1,0:T(8,128)(2,1)}, bf16[512,128]{1,0:T(8,128)(2,1)}, bf16[512,128]{1,0:T(8,128)(2,1)}) custom-call(bf16[4096,128]{1,0:T(8,128)(2,1)} %bitcast.4, bf16[512,128]{1,0:T(8,128)(2,1)} %k_hbm.1, bf16[512,128]{1,0:T(8,128)(2,1)} %v_hbm.1, bf16[4096,128]{1,0:T(8,128)(2,1)} %bitcast.5, s32[4,128]{1,0:T(4,128)} %bitcast.7), custom_call_target="tpu_custom_call" | custom-call | flops 10468982784 | bytes 4194304 | tf_op jit(solution)/shard_map/pallas_call | solution.py:335
  48.5 2.4 %shard_map.77 = (bf16[4096,128]{1,0:T(8,128)(2,1)}, bf16[512,128]{1,0:T(8,128)(2,1)}, bf16[512,128]{1,0:T(8,128)(2,1)}) custom-call(bf16[4096,128]{1,0:T(8,128)(2,1)} %get-tuple-element.9.dq_in, bf16[512,128]{1,0:T(8,128)(2,1)} %get-tuple-element.10.dk_in, bf16[512,128]{1,0:T(8,128)(2,1)} %get-tuple-element.11.dv_in), custom_call_target="tpu_custom_call" | custom-call | tf_op jit(solution)/shard_map/pallas_call | solution.py:385

commit v4 on v3

--- a/solution.py
+++ b/solution.py
@@ -322,9 +322,13 @@
         forward(2, d).wait_send()
 
 
-def finish(dq_in, dk_in, dv_in, dq_out, dk_out, dv_out):
-    for taken, given in ((dq_in, dq_out), (dk_in, dk_out), (dv_in, dv_out)):
-        given[...] = taken[...]
+def finish(dq_in, dk_in, dv_in, dq_out, dk_out, dv_out, sems):
+    pairs = ((dq_in, dq_out), (dk_in, dk_out), (dv_in, dv_out))
+    copies = [pltpu.make_async_copy(taken, given, sems.at[i]) for i, (taken, given) in enumerate(pairs)]
+    for copy in copies:
+        copy.start()
+    for copy in copies:
+        copy.wait()
 
 
 def local(outer, inner, queries, keys, values, grad_out, doc_ids):
@@ -390,7 +394,8 @@
             jax.ShapeDtypeStruct((tokens, width), BF),
         ),
         in_specs=[pl.BlockSpec(memory_space=vmem)] * 3,
-        out_specs=[pl.BlockSpec(memory_space=vmem)] * 3,
+        out_specs=[pl.BlockSpec(memory_space=pl.ANY)] * 3,
+        scratch_shapes=[pltpu.SemaphoreType.DMA((3,))],
     )(grad_queries, grad_keys, grad_values)
     return grad_queries.reshape(queries.shape), grad_keys, grad_values
 

time: 51.1 us -> 51.2 us (level)
  no operation moved by 1% of the time
where the time goes in v4:
time: 51.2 us; the launch traced here: 51.1 us
  Pallas kernels  50.3 us (98%)
  between operations  0.8 us (2%)
    pallas_call x1, Pallas kernels, local(): pl.pallas_call(functools.partial(kernel, outer, inner), out_shape=(jax.Sh...  47.9 us
    pallas_call x1, Pallas kernels, local(): pl.pallas_call(finish, out_shape=(jax.ShapeDtypeStruct((rows, width), BF)...  2.37 us

profile of v4, /device:TPU:0, one launch (start us, length us, event | category | flops | bytes accessed | tf_op | source)
XLA Modules:
  0.0 51.1 jit_solution(3450483338034871533)
XLA Ops:
  0.6 47.9 %shard_map.76 = (bf16[4096,128]{1,0:T(8,128)(2,1)}, bf16[512,128]{1,0:T(8,128)(2,1)}, bf16[512,128]{1,0:T(8,128)(2,1)}) custom-call(bf16[4096,128]{1,0:T(8,128)(2,1)} %bitcast.4, bf16[512,128]{1,0:T(8,128)(2,1)} %k_hbm.1, bf16[512,128]{1,0:T(8,128)(2,1)} %v_hbm.1, bf16[4096,128]{1,0:T(8,128)(2,1)} %bitcast.5, s32[4,128]{1,0:T(4,128)} %bitcast.7), custom_call_target="tpu_custom_call" | custom-call | flops 10468982784 | bytes 4194304 | tf_op jit(solution)/shard_map/pallas_call | solution.py:339
  48.5 2.4 %shard_map.77 = (bf16[4096,128]{1,0:T(8,128)(2,1)}, bf16[512,128]{1,0:T(8,128)(2,1)}, bf16[512,128]{1,0:T(8,128)(2,1)}) custom-call(bf16[4096,128]{1,0:T(8,128)(2,1)} %get-tuple-element.9.dq_in, bf16[512,128]{1,0:T(8,128)(2,1)} %get-tuple-element.10.dk_in, bf16[512,128]{1,0:T(8,128)(2,1)} %get-tuple-element.11.dv_in), custom_call_target="tpu_custom_call" | custom-call | tf_op jit(solution)/shard_map/pallas_call | solution.py:389
